TPU v7x, 32 devices: a whole 2x2x4 slice. The times are simulated.
32 devices in a mesh: work: 8 (over z, y), rep: 4 (over x, core).
Axes of the slice: x: 2, y: 2, z: 4, core: 2. Of those that a mesh axis runs over, the one named last changes fastest.
Arguments:
- gradients: bfloat16 [256, 512, 512], P('work', None, 'rep'), may hold values from -6 to 6
- output_stats: bfloat16 [8, 128, 512], P('work', 'rep'), may hold values from -6 to 6
- input_stats: bfloat16 [8, 128, 512], P('work', 'rep'), may hold values from -6 to 6
- output_factor: float32 [8, 512, 512], P('work')
- output_inverse: float32 [8, 512, 512], P('work')
- input_factor: float32 [8, 512, 512], P('work')
- input_inverse: float32 [8, 512, 512], P('work')
- block_output: int32 [256], replicated, may hold values from 0 to 7, as said below
- block_input: int32 [256], replicated, may hold values from 0 to 7, as said below
- output_owner: int32 [8], replicated, may hold values from 0 to 7, each once
- input_owner: int32 [8], replicated, may hold values from 0 to 7, each once
Outputs:
- preconditioned: bfloat16 [256, 512, 512], P('work', 'rep')
Inputs may be any that keep to these rules, and one draw needn't show every extreme that they name: `block_output`: among the 32 blocks of one home, no output factor is named more than 4 times, and some factor is named exactly 4 times; the same holds for input factors. No pair of an output factor and an input factor is named by more than 4 blocks in all. Every output factor and every input factor is named by exactly 32 blocks in all. `block_input`: drawn together with block_output; see there.
All inputs are finite; a program needn't handle non-finite values.
Results may differ from a plain program's by a relative error of at most 0.0067.
Values may be sent and summed in bfloat16 or wider, within the bound.
A program may use at most 128 MiB of HBM per device.

v0:
```python
import functools

import jax
import jax.numpy as jnp
from jax import lax
from jax.experimental import pallas as pl
from jax.experimental.pallas import tpu as pltpu
from jax.sharding import PartitionSpec as P

decay_rate = 0.5


def refine(factor, inverse, samples):
    moment = jnp.dot(samples.T, samples, preferred_element_type=jnp.float32)
    updated = decay_rate * factor + (1.0 - decay_rate) / samples.shape[0] * moment
    product = jnp.dot(updated, inverse, precision=lax.Precision.HIGHEST)
    refined = 2.0 * inverse - jnp.dot(inverse, product, precision=lax.Precision.HIGHEST)
    return refined.astype(jnp.bfloat16)


def lookup(labels, values):
    matches = labels[:, None] == jnp.arange(values.shape[0], dtype=jnp.int32)[None, :]
    return jnp.sum(jnp.where(matches, values[None, :], 0), axis=1)


def group_rank(grouping):
    count = grouping.shape[0]
    positions = jnp.arange(count, dtype=jnp.int32)
    same_group = grouping[:, None] == grouping[None, :]
    earlier = positions[None, :] < positions[:, None]
    return jnp.sum(jnp.logical_and(same_group, earlier), axis=1)


def place_rows(target, data, out_count):
    selector = (jnp.arange(out_count, dtype=jnp.int32)[:, None] == target[None, :]).astype(
        jnp.bfloat16
    )
    return jnp.einsum("st,tij->sij", selector, data, preferred_element_type=jnp.float32).astype(
        jnp.bfloat16
    )


def pick_rows(source, data):
    selector = (source[:, None] == jnp.arange(data.shape[0], dtype=jnp.int32)[None, :]).astype(
        jnp.bfloat16
    )
    return jnp.einsum("st,tij->sij", selector, data, preferred_element_type=jnp.float32).astype(
        jnp.bfloat16
    )


def redirect(slot_count, holding, source_slot, target_slot):
    chosen = jnp.where(holding, source_slot, slot_count)
    return jnp.full((slot_count,), slot_count, jnp.int32).at[chosen].set(target_slot, mode="drop")


def relocate(buffer, target, slot_count):
    flat_view = buffer.reshape((slot_count,) + buffer.shape[2:])
    placed = place_rows(target, flat_view, slot_count)
    return placed.reshape(buffer.shape)


def exchange_blocks(
    gradients,
    output_stats,
    input_stats,
    output_factor,
    output_inverse,
    input_factor,
    input_inverse,
    block_output,
    block_input,
    output_owner,
    input_owner,
):
    workers = lax.axis_size("work")
    local_blocks, block_order, shard_cols = gradients.shape
    total_blocks = block_output.shape[0]
    capacity = (local_blocks + workers - 1) // workers
    slot_count = workers * capacity
    worker_index = lax.axis_index("work")
    home_index = jnp.arange(total_blocks, dtype=jnp.int32) // local_blocks
    out_dest = lookup(block_output, output_owner)
    in_dest = lookup(block_input, input_owner)
    first_rank = group_rank(home_index * workers + out_dest)
    second_rank = group_rank(out_dest * workers + in_dest)
    third_rank = group_rank(in_dest * workers + home_index)
    gathered_out, gathered_in = (
        lax.all_gather(output_stats, "rep", axis=1, tiled=True),
        lax.all_gather(input_stats, "rep", axis=1, tiled=True),
    )
    left_inverse = refine(output_factor[0], output_inverse[0], gathered_out[0])
    right_inverse = refine(input_factor[0], input_inverse[0], gathered_in[0])
    own_places = lax.dynamic_slice_in_dim(
        out_dest * capacity + first_rank, worker_index * local_blocks, local_blocks
    )
    outgoing = place_rows(own_places, gradients, slot_count)
    outgoing = outgoing.reshape(workers, capacity, block_order, shard_cols)
    arrived = jnp.einsum(
        "ij,nkjc->nkic",
        left_inverse,
        lax.all_to_all(outgoing, "work", split_axis=0, concat_axis=0, tiled=True),
        preferred_element_type=jnp.float32,
    ).astype(jnp.bfloat16)
    second_target = redirect(
        slot_count,
        out_dest == worker_index,
        home_index * capacity + first_rank,
        in_dest * capacity + second_rank,
    )
    forward = relocate(arrived, second_target, slot_count)
    third_target = redirect(
        slot_count,
        in_dest == worker_index,
        out_dest * capacity + second_rank,
        home_index * capacity + third_rank,
    )
    rows_form = lax.all_to_all(forward, "rep", split_axis=2, concat_axis=3, tiled=True)
    finished = jnp.einsum(
        "nkrc,cd->nkrd",
        lax.all_to_all(rows_form, "work", split_axis=0, concat_axis=0, tiled=True),
        right_inverse,
        preferred_element_type=jnp.float32,
    ).astype(jnp.bfloat16)
    backward = relocate(finished, third_target, slot_count)
    returned = lax.all_to_all(backward, "work", split_axis=0, concat_axis=0, tiled=True)
    returned = returned.reshape((slot_count,) + returned.shape[2:])
    own_slots = lax.dynamic_slice_in_dim(
        in_dest * capacity + third_rank, worker_index * local_blocks, local_blocks
    )
    return pick_rows(own_slots, returned)


def flip(value, mask):
    result, bit = value, 1
    while bit <= mask:
        if mask & bit:
            result = result + bit - 2 * bit * ((value // bit) % 2)
        bit *= 2
    return result


def halves(x):
    high = x.astype(jnp.bfloat16)
    return high, (x - high.astype(jnp.float32)).astype(jnp.bfloat16)


def dot(a, b):
    return jnp.dot(a, b, preferred_element_type=jnp.float32)


def exact_dot(a, b):
    return dot(a[0], b[0]) + (dot(a[0], b[1]) + dot(a[1], b[0]))


def fused_kernel(
    workers,
    replicas,
    first_ref,
    second_ref,
    g_ref,
    os_ref,
    is_ref,
    of_ref,
    oi_ref,
    if_ref,
    ii_ref,
    out_ref,
    stats,
    factors,
    middle,
    rows,
    result,
    stat_send,
    stat_recv,
    z_send,
    z_recv,
    y_send,
    y_recv,
    s_send,
    s_recv,
    m_send,
    m_recv,
    out_sem,
):
    work, rep = lax.axis_index("work"), lax.axis_index("rep")
    blocks, order, cols = g_ref.shape
    capacity = blocks // workers
    lines = workers // 2
    share = order // replicas
    half = order // 2
    core = rep % 2
    sibling = {"rep": flip(rep, 1)}
    pending = []

    barrier = pltpu.get_barrier_semaphore()
    peers = [{"rep": flip(rep, d)} for d in range(1, replicas)]
    peers += [{"work": flip(work, 1)}] + [{"work": flip(work, 2 * d)} for d in range(1, lines)]
    for peer in peers:
        pl.semaphore_signal(barrier, inc=1, device_id=peer, device_id_type=pl.DeviceIdType.MESH)
    pl.semaphore_wait(barrier, len(peers))

    def push(src, dst, send, recv, peer):
        copy = pltpu.make_async_remote_copy(
            src_ref=src,
            dst_ref=dst,
            send_sem=send,
            recv_sem=recv,
            device_id=peer,
            device_id_type=pl.DeviceIdType.MESH,
        )
        copy.start()
        pending.append(copy)
        return copy

    stat_copies = []
    for t, ref in enumerate((os_ref, is_ref)):
        for d in range(1, replicas):
            stat_copies.append(
                push(
                    ref.at[0],
                    stats.at[t, rep],
                    stat_send.at[t, d - 1],
                    stat_recv.at[t, d - 1],
                    {"rep": flip(rep, d)},
                )
            )
        stats[t, rep] = ref[0]

    mine = pl.ds(pl.multiple_of(core * half, half), half)
    places = [flip(work, i) for i in range(workers)]

    def chunk(t, i):
        return factors.at[t, places[i], mine]

    def refine_half(t, f_ref, i_ref):
        for copy in stat_copies[t * (replicas - 1) : (t + 1) * (replicas - 1)]:
            copy.wait_recv()
        sample = stats[t].reshape(-1, order)
        moment = lax.dot_general(
            sample, sample, (((0,), (0,)), ((), ())), preferred_element_type=jnp.float32
        )
        updated = decay_rate * f_ref[0] + (1.0 - decay_rate) / sample.shape[0] * moment
        own = i_ref[0, mine]
        product = exact_dot(halves(own), halves(updated))
        refined = 2.0 * own - exact_dot(halves(product), halves(i_ref[0]))
        factors[t, places[0], mine] = refined.astype(jnp.bfloat16)

    z_copies, y_copies, s_copies = {}, {}, {}

    def to_sibling(t, i):
        s_copies[t, i] = push(chunk(t, i), chunk(t, i), s_send.at[t, i], s_recv.at[t, i], sibling)

    def to_y(t, d):
        y_copies[t, d] = push(
            chunk(t, 2 * d),
            chunk(t, 2 * d),
            y_send.at[t, d],
            y_recv.at[t, d],
            {"work": places[1]},
        )

    def to_z(t):
        for d in range(1, lines):
            z_copies[t, d] = push(
                chunk(t, 0),
                chunk(t, 0),
                z_send.at[t, d - 1],
                z_recv.at[t, d - 1],
                {"work": places[2 * d]},
            )

    m_copies = []
    own_cols = pl.ds(pl.multiple_of(rep * cols, cols), cols)
    own_rows = pl.ds(pl.multiple_of(rep * share, share), share)

    def left_multiply(i):
        slots = pl.ds(i * capacity, capacity)
        wide = jnp.concatenate(
            [g_ref[first_ref[i * capacity + k]] for k in range(capacity)], axis=1
        )
        for j in range(2):
            part = pl.ds(j * half, half)
            product = dot(factors[0, places[i], part], wide).astype(jnp.bfloat16)
            for k in range(capacity):
                middle[i * capacity + k, part] = product[:, k * cols : (k + 1) * cols]
        for d in range(replicas - 1, 0, -1):
            other = flip(rep, d)
            m_copies.append(
                push(
                    middle.at[slots, pl.ds(pl.multiple_of(other * share, share), share)],
                    rows.at[slots, :, own_cols],
                    m_send.at[i, d - 1],
                    m_recv.at[i, d - 1],
                    {"rep": other},
                )
            )
        rows[slots, :, own_cols] = middle[slots, own_rows]

    def spread(t, ready):
        done = 0
        queue = [0]
        for d in range(1, lines + 1):
            if d < lines:
                z_copies[t, d].wait_recv()
                to_y(t, d)
                to_sibling(t, 2 * d)
                if d == lines - 1 and t == 0:
                    to_y(1, 0)
                    to_z(1)
                    to_sibling(1, 0)
            while queue:
                i = queue.pop(0)
                s_copies[t, i].wait_recv()
                ready(i)
            y_copies[t, d - 1].wait_recv()
            to_sibling(t, 2 * d - 1)
            if d < lines:
                queue.append(2 * d)
            queue.append(2 * d - 1)
        for i in queue:
            s_copies[t, i].wait_recv()
            ready(i)

    refine_half(0, of_ref, oi_ref)
    to_y(0, 0)
    to_z(0)
    to_sibling(0, 0)
    refine_half(1, if_ref, ii_ref)
    spread(0, left_multiply)
    whole = []
    spread(1, whole.append)
    for copy in m_copies:
        copy.wait_recv()
    out_copies = []
    for i in range(workers):
        slots = pl.ds(i * capacity, capacity)
        for k in range(0, capacity, 2):
            pair = [rows[second_ref[i * capacity + k + j]] for j in range(min(2, capacity - k))]
            product = dot(jnp.concatenate(pair, axis=0), factors[1, places[i]])
            for j in range(len(pair)):
                result[i * capacity + k + j] = product[j * share : (j + 1) * share].astype(
                    jnp.bfloat16
                )
        copy = pltpu.make_async_copy(result.at[slots], out_ref.at[slots], out_sem.at[i])
        copy.start()
        out_copies.append(copy)
    for copy in out_copies:
        copy.wait()
    for copy in pending:
        copy.wait_send()


def permute_kernel(place_ref, in_ref, out_ref, sems):
    copies = []
    for b in range(in_ref.shape[0]):
        copy = pltpu.make_async_copy(in_ref.at[place_ref[b]], out_ref.at[b], sems.at[b])
        copy.start()
        copies.append(copy)
    for copy in copies:
        copy.wait()


def gather_factors(
    gradients,
    output_stats,
    input_stats,
    output_factor,
    output_inverse,
    input_factor,
    input_inverse,
    block_output,
    block_input,
    output_owner,
    input_owner,
):
    workers, replicas = lax.axis_size("work"), lax.axis_size("rep")
    blocks, order, cols = gradients.shape
    capacity = blocks // workers
    share = order // replicas
    work = lax.axis_index("work")
    labels = jnp.stack([block_output, block_input]).reshape(2, workers, blocks)
    labels = lax.dynamic_index_in_dim(labels, work, 1, keepdims=False)
    owners = jnp.stack([output_owner, input_owner]) ^ work
    choices = jnp.arange(owners.shape[1], dtype=jnp.int32)
    dest = jnp.sum(jnp.where(labels[:, :, None] == choices, owners[:, None, :], 0), axis=2)
    at = jnp.arange(blocks, dtype=jnp.int32)
    same = (dest[:, :, None] == dest[:, None, :]) & (at[None, :] < at[:, None])
    slot = dest * capacity + jnp.sum(same, axis=2)
    held = slot[:, None, :] == at[:, None]
    first = jnp.sum(jnp.where(held[0], at, 0), axis=1)
    second = jnp.sum(jnp.where(held[1], slot[0], 0), axis=1)
    smem = pl.BlockSpec(memory_space=pltpu.SMEM)
    vmem = pl.BlockSpec(memory_space=pltpu.VMEM)
    hbm = pl.BlockSpec(memory_space=pl.ANY)
    sem = pltpu.SemaphoreType.DMA
    lines = workers // 2
    bf16 = jnp.bfloat16
    result = pl.pallas_call(
        functools.partial(fused_kernel, workers, replicas),
        out_shape=jax.ShapeDtypeStruct((blocks, share, order), bf16),
        in_specs=[smem] * 2 + [vmem] * 7,
        out_specs=hbm,
        scratch_shapes=[
            pltpu.VMEM((2, replicas) + output_stats.shape[1:], bf16),
            pltpu.VMEM((2, workers, order, order), bf16),
            pltpu.VMEM((blocks, order, cols), bf16),
            pltpu.VMEM((blocks, share, order), bf16),
            pltpu.VMEM((blocks, share, order), bf16),
            sem((2, replicas - 1)),
            sem((2, replicas - 1)),
            sem((2, lines - 1)),
            sem((2, lines - 1)),
            sem((2, lines)),
            sem((2, lines)),
            sem((2, workers)),
            sem((2, workers)),
            sem((workers, replicas - 1)),
            sem((workers, replicas - 1)),
            sem((workers,)),
        ],
        compiler_params=pltpu.CompilerParams(
            collective_id=0, has_side_effects=True, vmem_limit_bytes=50 * 1024 * 1024
        ),
    )(
        first,
        second,
        gradients,
        output_stats,
        input_stats,
        output_factor,
        output_inverse,
        input_factor,
        input_inverse,
    )
    return pl.pallas_call(
        permute_kernel,
        out_shape=jax.ShapeDtypeStruct((blocks, share, order), bf16),
        in_specs=[smem, hbm],
        out_specs=hbm,
        scratch_shapes=[sem((blocks,))],
    )(slot[1], result)


def solution(mesh):
    in_specs = (
        P("work", None, "rep"),
        P("work", "rep", None),
        P("work", "rep", None),
        P("work", None, None),
        P("work", None, None),
        P("work", None, None),
        P("work", None, None),
        P(),
        P(),
        P(),
        P(),
    )
    out_specs = P("work", "rep", None)
    workers, replicas = mesh.shape["work"], mesh.shape["rep"]
    small = 4 <= workers <= 8 and replicas in (2, 4)
    local = gather_factors if small else exchange_blocks
    return jax.shard_map(local, mesh=mesh, in_specs=in_specs, out_specs=out_specs, check_vma=False)
```

profile of v0, /device:TPU:0, one launch (start us, length us, event | category | flops | bytes accessed | tf_op | source)
XLA Modules:
  0.0 213.8 jit_solution(17321220294898680597)
XLA Ops:
  0.0 0.7 add_xor_fusion
  0.7 0.8 stack.18
  1.4 0.8 stack.19
  2.2 0.1 select_reduce_fusion.2
  2.3 0.2 convert_reduce_fusion
  2.5 0.5 slice_bitcast_fusion.2
  3.0 0.1 select_reduce_fusion
  3.2 0.0 copy-start
  3.2 1.2 copy-done
  4.4 0.0 copy-start.1
  4.4 1.2 copy-done.1
  5.6 0.0 copy-start.2
  5.6 1.2 copy-done.2
  6.8 0.0 copy-start.3
  6.8 0.8 copy-done.3
  7.6 0.0 copy-start.4
  7.6 0.8 copy-done.4
  8.4 76.3 %shard_map.109.in_ref = bf16[32,128,512]{2,1,0:T(8,128)(2,1)} custom-call(s32[32]{0:T(128)S(1)} %get-tuple-element.6.first_ref, s32[32]{0:T(128)S(1)} %get-tuple-element.5.second_ref, bf16[32,512,128]{2,1,0:T(8,128)(2,1)} %g_ref.1, bf16[1,32,512]{2,1,0:T(8,128)(2,1)S(1)} %copy-done.3, bf16[1,32,512]{2,1,0:T(8,128)(2,1)S(1)} %copy-done.4, ...), custom_call_target="tpu_custom_call" | custom-call | tf_op jit(solution)/shard_map/pallas_call | solution.py:399
  84.7 129.1 %shard_map.110 = bf16[32,128,512]{2,1,0:T(8,128)(2,1)} custom-call(s32[32]{0:T(128)} %get-tuple-element.8.place_ref, bf16[32,128,512]{2,1,0:T(8,128)(2,1)} %shard_map.109.in_ref), custom_call_target="tpu_custom_call" | custom-call | tf_op jit(solution)/shard_map/pallas_call | solution.py:436
  (4 shorter events, 0.0 us)
Async XLA Ops:
  3.2 1.2 copy-start
  4.4 1.2 copy-start.1
  5.6 1.2 copy-start.2
  6.8 0.8 copy-start.3
  7.6 0.8 copy-start.4
where the time goes:
time: 214 us
  Pallas kernels  205 us (96%)
  local copies, waits for them, and re-layouts  7.24 us (3%)
    pallas_call x1, Pallas kernels, gather_factors(): pl.pallas_call(permute_kernel, out_shape=jax.ShapeDtypeStruct((blocks, sh...  129 us
    pallas_call x1, Pallas kernels, gather_factors(): pl.pallas_call(functools.partial(fused_kernel, workers, replicas), out_sh...  76.3 us
    unnamed x10, local copies, waits for them, and re-layouts  5.19 us

commit v1 on v0

--- a/solution.py
+++ b/solution.py
@@ -158,14 +158,19 @@
     replicas,
     first_ref,
     second_ref,
-    g_ref,
+    g_hbm,
     os_ref,
     is_ref,
+    of_hbm,
+    oi_hbm,
+    if_hbm,
+    ii_hbm,
+    out_ref,
+    g_ref,
     of_ref,
     oi_ref,
     if_ref,
     ii_ref,
-    out_ref,
     stats,
     factors,
     middle,
@@ -182,6 +187,7 @@
     m_send,
     m_recv,
     out_sem,
+    load_sem,
 ):
     work, rep = lax.axis_index("work"), lax.axis_index("rep")
     blocks, order, cols = g_ref.shape
@@ -192,6 +198,13 @@
     core = rep % 2
     sibling = {"rep": flip(rep, 1)}
     pending = []
+
+    sources = (of_hbm, oi_hbm, if_hbm, ii_hbm, g_hbm)
+    targets = (of_ref, oi_ref, if_ref, ii_ref, g_ref)
+    loads = []
+    for n, (source, target) in enumerate(zip(sources, targets)):
+        loads.append(pltpu.make_async_copy(source, target, load_sem.at[n]))
+        loads[n].start()
 
     barrier = pltpu.get_barrier_semaphore()
     peers = [{"rep": flip(rep, d)} for d in range(1, replicas)]
@@ -236,6 +249,8 @@
     def refine_half(t, f_ref, i_ref):
         for copy in stat_copies[t * (replicas - 1) : (t + 1) * (replicas - 1)]:
             copy.wait_recv()
+        loads[2 * t].wait()
+        loads[2 * t + 1].wait()
         sample = stats[t].reshape(-1, order)
         moment = lax.dot_general(
             sample, sample, (((0,), (0,)), ((), ())), preferred_element_type=jnp.float32
@@ -298,8 +313,7 @@
         rows[slots, :, own_cols] = middle[slots, own_rows]
 
     def spread(t, ready):
-        done = 0
-        queue = [0]
+        queue = []
         for d in range(1, lines + 1):
             if d < lines:
                 z_copies[t, d].wait_recv()
@@ -326,10 +340,13 @@
     to_y(0, 0)
     to_z(0)
     to_sibling(0, 0)
+    loads[4].wait()
+    s_copies[0, 0].wait_recv()
+    left_multiply(0)
     refine_half(1, if_ref, ii_ref)
     spread(0, left_multiply)
-    whole = []
-    spread(1, whole.append)
+    s_copies[1, 0].wait_recv()
+    spread(1, lambda i: None)
     for copy in m_copies:
         copy.wait_recv()
     out_copies = []
@@ -351,13 +368,20 @@
         copy.wait_send()
 
 
-def permute_kernel(place_ref, in_ref, out_ref, sems):
-    copies = []
-    for b in range(in_ref.shape[0]):
-        copy = pltpu.make_async_copy(in_ref.at[place_ref[b]], out_ref.at[b], sems.at[b])
-        copy.start()
-        copies.append(copy)
-    for copy in copies:
+def permute_kernel(place_ref, in_ref, out_ref, buffer, in_sems, out_sems):
+    blocks = in_ref.shape[0]
+    loads = []
+    for b in range(blocks):
+        loads.append(
+            pltpu.make_async_copy(in_ref.at[place_ref[b]], buffer.at[b], in_sems.at[b])
+        )
+        loads[b].start()
+    stores = []
+    for b in range(blocks):
+        loads[b].wait()
+        stores.append(pltpu.make_async_copy(buffer.at[b], out_ref.at[b], out_sems.at[b]))
+        stores[b].start()
+    for copy in stores:
         copy.wait()
 
 
@@ -379,17 +403,19 @@
     capacity = blocks // workers
     share = order // replicas
     work = lax.axis_index("work")
-    labels = jnp.stack([block_output, block_input]).reshape(2, workers, blocks)
-    labels = lax.dynamic_index_in_dim(labels, work, 1, keepdims=False)
-    owners = jnp.stack([output_owner, input_owner]) ^ work
-    choices = jnp.arange(owners.shape[1], dtype=jnp.int32)
-    dest = jnp.sum(jnp.where(labels[:, :, None] == choices, owners[:, None, :], 0), axis=2)
     at = jnp.arange(blocks, dtype=jnp.int32)
-    same = (dest[:, :, None] == dest[:, None, :]) & (at[None, :] < at[:, None])
-    slot = dest * capacity + jnp.sum(same, axis=2)
-    held = slot[:, None, :] == at[:, None]
-    first = jnp.sum(jnp.where(held[0], at, 0), axis=1)
-    second = jnp.sum(jnp.where(held[1], slot[0], 0), axis=1)
+
+    def slots_of(labels, owner):
+        labels = lax.dynamic_slice_in_dim(labels, work * blocks, blocks)
+        dest = lookup(labels, owner ^ work)
+        return dest * capacity + group_rank(dest)
+
+    def by_slot(slot, values):
+        return jnp.sum(jnp.where(slot[None, :] == at[:, None], values[None, :], 0), axis=1)
+
+    out_slot = slots_of(block_output, output_owner)
+    in_slot = slots_of(block_input, input_owner)
+    first, second = by_slot(out_slot, at), by_slot(in_slot, out_slot)
     smem = pl.BlockSpec(memory_space=pltpu.SMEM)
     vmem = pl.BlockSpec(memory_space=pltpu.VMEM)
     hbm = pl.BlockSpec(memory_space=pl.ANY)
@@ -399,9 +425,14 @@
     result = pl.pallas_call(
         functools.partial(fused_kernel, workers, replicas),
         out_shape=jax.ShapeDtypeStruct((blocks, share, order), bf16),
-        in_specs=[smem] * 2 + [vmem] * 7,
+        in_specs=[smem] * 2 + [hbm] + [vmem] * 2 + [hbm] * 4,
         out_specs=hbm,
         scratch_shapes=[
+            pltpu.VMEM(gradients.shape, bf16),
+            pltpu.VMEM(output_factor.shape, jnp.float32),
+            pltpu.VMEM(output_inverse.shape, jnp.float32),
+            pltpu.VMEM(input_factor.shape, jnp.float32),
+            pltpu.VMEM(input_inverse.shape, jnp.float32),
             pltpu.VMEM((2, replicas) + output_stats.shape[1:], bf16),
             pltpu.VMEM((2, workers, order, order), bf16),
             pltpu.VMEM((blocks, order, cols), bf16),
@@ -418,9 +449,10 @@
             sem((workers, replicas - 1)),
             sem((workers, replicas - 1)),
             sem((workers,)),
+            sem((5,)),
         ],
         compiler_params=pltpu.CompilerParams(
-            collective_id=0, has_side_effects=True, vmem_limit_bytes=50 * 1024 * 1024
+            collective_id=0, has_side_effects=True, vmem_limit_bytes=58 * 1024 * 1024
         ),
     )(
         first,
@@ -438,8 +470,13 @@
         out_shape=jax.ShapeDtypeStruct((blocks, share, order), bf16),
         in_specs=[smem, hbm],
         out_specs=hbm,
-        scratch_shapes=[sem((blocks,))],
-    )(slot[1], result)
+        scratch_shapes=[
+            pltpu.VMEM((blocks, share, order), bf16),
+            sem((blocks,)),
+            sem((blocks,)),
+        ],
+        compiler_params=pltpu.CompilerParams(vmem_limit_bytes=56 * 1024 * 1024),
+    )(in_slot, result)
 
 
 def solution(mesh):

time: 214 us -> 81.2 us (0.38)
  Pallas kernels: 205 us -> 76.4 us
  local copies, waits for them, and re-layouts: 7.24 us -> 1.51 us
    pallas_call x1, Pallas kernels: 129 us -> 5.18 us  [gather_factors(): pl.pallas_call(permute_kernel, out_shape=jax.ShapeDtypeStruct((blocks, sh...]
    unnamed x10 -> x2, local copies, waits for them, and re-layouts: 5.19 us -> 0.01 us
    pallas_call x1, Pallas kernels: 76.3 us -> 71.2 us  [gather_factors(): pl.pallas_call(functools.partial(fused_kernel, workers, replicas), out_sh...]
where the time goes in v1:
time: 81.2 us; the launch traced here: 79.8 us
  Pallas kernels  76.4 us (94%)
  other arithmetic  1.89 us (2%)
  local copies, waits for them, and re-layouts  1.51 us (2%)
    pallas_call x1, Pallas kernels, gather_factors(): pl.pallas_call(functools.partial(fused_kernel, workers, replicas), out_sh...  71.2 us
    pallas_call x1, Pallas kernels, gather_factors(): pl.pallas_call(permute_kernel, out_shape=jax.ShapeDtypeStruct((blocks, sh...  5.18 us

profile of v1, /device:TPU:0, one launch (start us, length us, event | category | flops | bytes accessed | tf_op | source)
XLA Modules:
  0.0 79.8 jit_solution(2300812056576762705)
XLA Ops:
  0.0 0.8 dynamic_slice.7
  0.8 0.8 dynamic_slice.6
  1.5 0.7 broadcast_xor_fusion
  2.2 0.1 select_reduce_fusion.2
  2.3 0.1 select_reduce_fusion.3
  2.3 0.2 convert_reduce_fusion.1
  2.5 0.0 copy-start
  2.5 0.2 convert_reduce_fusion
  2.7 0.7 select_reduce_fusion
  3.4 71.2 %shard_map.109.in_ref = bf16[32,128,512]{2,1,0:T(8,128)(2,1)} custom-call(s32[32]{0:T(128)} %get-tuple-element.6.first_ref, s32[32]{0:T(128)} %get-tuple-element.5.second_ref, bf16[32,512,128]{2,1,0:T(8,128)(2,1)} %g_hbm.1, bf16[1,32,512]{2,1,0:T(8,128)(2,1)} %os_ref.1, bf16[1,32,512]{2,1,0:T(8,128)(2,1)} %is_ref.1, f32[1,512,512]{2,1,0:T(8,128)} %of_hbm.1, ...), custom_call_target="tpu_custom_call" | custom-call | tf_op jit(solution)/shard_map/pallas_call | solution.py:425
  74.6 0.0 copy-done
  74.6 5.2 %shard_map.110 = bf16[32,128,512]{2,1,0:T(8,128)(2,1)} custom-call(s32[32]{0:T(128)} %copy-done, bf16[32,128,512]{2,1,0:T(8,128)(2,1)} %shard_map.109.in_ref), custom_call_target="tpu_custom_call" | custom-call | tf_op jit(solution)/shard_map/pallas_call | solution.py:468
  (2 shorter events, 0.0 us)
Async XLA Ops:
  2.5 72.1 %copy-start = (s32[32]{0:T(128)}, s32[32]{0:T(128)S(1)}, u32[]{:S(2)}) copy-start(s32[32]{0:T(128)S(1)} %multiply_add_fusion.1.place_ref) | copy-start | bytes 388

commit v2 on v1

--- a/solution.py
+++ b/solution.py
@@ -312,17 +312,18 @@
             )
         rows[slots, :, own_cols] = middle[slots, own_rows]
 
-    def spread(t, ready):
+    def spread_left(t, ready):
         queue = []
         for d in range(1, lines + 1):
             if d < lines:
                 z_copies[t, d].wait_recv()
                 to_y(t, d)
                 to_sibling(t, 2 * d)
-                if d == lines - 1 and t == 0:
+                if d == 1:
                     to_y(1, 0)
+                    to_sibling(1, 0)
+                if d == lines // 2:
                     to_z(1)
-                    to_sibling(1, 0)
             while queue:
                 i = queue.pop(0)
                 s_copies[t, i].wait_recv()
@@ -336,6 +337,17 @@
             s_copies[t, i].wait_recv()
             ready(i)
 
+    def spread_right(t):
+        for d in range(1, lines):
+            z_copies[t, d].wait_recv()
+            to_y(t, d)
+            to_sibling(t, 2 * d)
+        for d in range(lines):
+            y_copies[t, d].wait_recv()
+            to_sibling(t, 2 * d + 1)
+        for i in range(workers):
+            s_copies[t, i].wait_recv()
+
     refine_half(0, of_ref, oi_ref)
     to_y(0, 0)
     to_z(0)
@@ -344,9 +356,8 @@
     s_copies[0, 0].wait_recv()
     left_multiply(0)
     refine_half(1, if_ref, ii_ref)
-    spread(0, left_multiply)
-    s_copies[1, 0].wait_recv()
-    spread(1, lambda i: None)
+    spread_left(0, left_multiply)
+    spread_right(1)
     for copy in m_copies:
         copy.wait_recv()
     out_copies = []

time: 81.2 us -> 82.7 us (1.018); the launches traced: 79.8 us -> 82.5 us
  Pallas kernels: 76.4 us -> 79.1 us
    pallas_call x1, Pallas kernels: 71.2 us -> 73.9 us  [gather_factors(): pl.pallas_call(functools.partial(fused_kernel, workers, replicas), out_sh...]
where the time goes in v2:
time: 82.7 us; the launch traced here: 82.5 us
  Pallas kernels  79.1 us (96%)
  other arithmetic  1.89 us (2%)
  local copies, waits for them, and re-layouts  1.51 us (2%)
    pallas_call x1, Pallas kernels, gather_factors(): pl.pallas_call(functools.partial(fused_kernel, workers, replicas), out_sh...  73.9 us
    pallas_call x1, Pallas kernels, gather_factors(): pl.pallas_call(permute_kernel, out_shape=jax.ShapeDtypeStruct((blocks, sh...  5.18 us

profile of v2, /device:TPU:0, one launch (start us, length us, event | category | flops | bytes accessed | tf_op | source)
XLA Modules:
  0.0 82.5 jit_solution(71721628292265564)
XLA Ops:
  0.0 0.8 dynamic_slice.7
  0.8 0.8 dynamic_slice.6
  1.5 0.7 broadcast_xor_fusion
  2.2 0.1 select_reduce_fusion.2
  2.3 0.1 select_reduce_fusion.3
  2.3 0.2 convert_reduce_fusion.1
  2.5 0.0 copy-start
  2.5 0.2 convert_reduce_fusion
  2.7 0.7 select_reduce_fusion
  3.4 73.9 %shard_map.109.in_ref = bf16[32,128,512]{2,1,0:T(8,128)(2,1)} custom-call(s32[32]{0:T(128)} %get-tuple-element.6.first_ref, s32[32]{0:T(128)} %get-tuple-element.5.second_ref, bf16[32,512,128]{2,1,0:T(8,128)(2,1)} %g_hbm.1, bf16[1,32,512]{2,1,0:T(8,128)(2,1)} %os_ref.1, bf16[1,32,512]{2,1,0:T(8,128)(2,1)} %is_ref.1, f32[1,512,512]{2,1,0:T(8,128)} %of_hbm.1, ...), custom_call_target="tpu_custom_call" | custom-call | tf_op jit(solution)/shard_map/pallas_call | solution.py:436
  77.3 0.0 copy-done
  77.3 5.2 %shard_map.110 = bf16[32,128,512]{2,1,0:T(8,128)(2,1)} custom-call(s32[32]{0:T(128)} %copy-done, bf16[32,128,512]{2,1,0:T(8,128)(2,1)} %shard_map.109.in_ref), custom_call_target="tpu_custom_call" | custom-call | tf_op jit(solution)/shard_map/pallas_call | solution.py:479
  (2 shorter events, 0.0 us)
Async XLA Ops:
  2.5 74.8 %copy-start = (s32[32]{0:T(128)}, s32[32]{0:T(128)S(1)}, u32[]{:S(2)}) copy-start(s32[32]{0:T(128)S(1)} %multiply_add_fusion.1.place_ref) | copy-start | bytes 388

commit v3 on v1

--- a/solution.py
+++ b/solution.py
@@ -286,7 +286,6 @@
             )
 
     m_copies = []
-    own_cols = pl.ds(pl.multiple_of(rep * cols, cols), cols)
     own_rows = pl.ds(pl.multiple_of(rep * share, share), share)
 
     def left_multiply(i):
@@ -304,13 +303,13 @@
             m_copies.append(
                 push(
                     middle.at[slots, pl.ds(pl.multiple_of(other * share, share), share)],
-                    rows.at[slots, :, own_cols],
+                    rows.at[rep, slots],
                     m_send.at[i, d - 1],
                     m_recv.at[i, d - 1],
                     {"rep": other},
                 )
             )
-        rows[slots, :, own_cols] = middle[slots, own_rows]
+        rows[rep, slots] = middle[slots, own_rows]
 
     def spread(t, ready):
         queue = []
@@ -353,7 +352,10 @@
     for i in range(workers):
         slots = pl.ds(i * capacity, capacity)
         for k in range(0, capacity, 2):
-            pair = [rows[second_ref[i * capacity + k + j]] for j in range(min(2, capacity - k))]
+            pair = []
+            for j in range(min(2, capacity - k)):
+                place = second_ref[i * capacity + k + j]
+                pair.append(jnp.concatenate([rows[r, place] for r in range(replicas)], axis=1))
             product = dot(jnp.concatenate(pair, axis=0), factors[1, places[i]])
             for j in range(len(pair)):
                 result[i * capacity + k + j] = product[j * share : (j + 1) * share].astype(
@@ -436,7 +438,7 @@
             pltpu.VMEM((2, replicas) + output_stats.shape[1:], bf16),
             pltpu.VMEM((2, workers, order, order), bf16),
             pltpu.VMEM((blocks, order, cols), bf16),
-            pltpu.VMEM((blocks, share, order), bf16),
+            pltpu.VMEM((replicas, blocks, share, cols), bf16),
             pltpu.VMEM((blocks, share, order), bf16),
             sem((2, replicas - 1)),
             sem((2, replicas - 1)),

time: 81.2 us -> 81.2 us (level)
  no operation moved by 1% of the time
where the time goes in v3:
time: 81.2 us; the launch traced here: 79.8 us
  Pallas kernels  76.4 us (94%)
  other arithmetic  1.89 us (2%)
  local copies, waits for them, and re-layouts  1.51 us (2%)
    pallas_call x1, Pallas kernels, gather_factors(): pl.pallas_call(functools.partial(fused_kernel, workers, replicas), out_sh...  71.2 us
    pallas_call x1, Pallas kernels, gather_factors(): pl.pallas_call(permute_kernel, out_shape=jax.ShapeDtypeStruct((blocks, sh...  5.18 us

profile of v3, /device:TPU:0, one launch (start us, length us, event | category | flops | bytes accessed | tf_op | source)
XLA Modules:
  0.0 79.8 jit_solution(13929723356244796943)
XLA Ops:
  0.0 0.8 dynamic_slice.7
  0.8 0.8 dynamic_slice.6
  1.5 0.7 broadcast_xor_fusion
  2.2 0.1 select_reduce_fusion.2
  2.3 0.1 select_reduce_fusion.3
  2.3 0.2 convert_reduce_fusion.1
  2.5 0.0 copy-start
  2.5 0.2 convert_reduce_fusion
  2.7 0.7 select_reduce_fusion
  3.4 71.2 %shard_map.109.in_ref = bf16[32,128,512]{2,1,0:T(8,128)(2,1)} custom-call(s32[32]{0:T(128)} %get-tuple-element.6.first_ref, s32[32]{0:T(128)} %get-tuple-element.5.second_ref, bf16[32,512,128]{2,1,0:T(8,128)(2,1)} %g_hbm.1, bf16[1,32,512]{2,1,0:T(8,128)(2,1)} %os_ref.1, bf16[1,32,512]{2,1,0:T(8,128)(2,1)} %is_ref.1, f32[1,512,512]{2,1,0:T(8,128)} %of_hbm.1, ...), custom_call_target="tpu_custom_call" | custom-call | tf_op jit(solution)/shard_map/pallas_call | solution.py:427
  74.6 0.0 copy-done
  74.6 5.2 %shard_map.110 = bf16[32,128,512]{2,1,0:T(8,128)(2,1)} custom-call(s32[32]{0:T(128)} %copy-done, bf16[32,128,512]{2,1,0:T(8,128)(2,1)} %shard_map.109.in_ref), custom_call_target="tpu_custom_call" | custom-call | tf_op jit(solution)/shard_map/pallas_call | solution.py:470
  (2 shorter events, 0.0 us)
Async XLA Ops:
  2.5 72.1 %copy-start = (s32[32]{0:T(128)}, s32[32]{0:T(128)S(1)}, u32[]{:S(2)}) copy-start(s32[32]{0:T(128)S(1)} %multiply_add_fusion.1.place_ref) | copy-start | bytes 388

commit v4 on v3

--- a/solution.py
+++ b/solution.py
@@ -408,7 +408,8 @@
     at = jnp.arange(blocks, dtype=jnp.int32)
 
     def slots_of(labels, owner):
-        labels = lax.dynamic_slice_in_dim(labels, work * blocks, blocks)
+        homes = jnp.arange(workers, dtype=jnp.int32)[:, None]
+        labels = jnp.sum(jnp.where(homes == work, labels.reshape(workers, blocks), 0), axis=0)
         dest = lookup(labels, owner ^ work)
         return dest * capacity + group_rank(dest)
 

time: 81.2 us -> 81.3 us (level)
    reshape x0 -> x2, local copies, waits for them, and re-layouts: none -> 1.51 us  [slots_of(): labels.reshape(workers, blocks)]
    dynamic_slice x2 -> x0, local copies, waits for them, and re-layouts: 1.5 us -> none  [slots_of(): labels = lax.dynamic_slice_in_dim(labels, work * blocks, blocks)]
where the time goes in v4:
time: 81.3 us; the launch traced here: 79.9 us
  Pallas kernels  76.4 us (94%)
  other arithmetic  1.98 us (2%)
  local copies, waits for them, and re-layouts  1.51 us (2%)
    pallas_call x1, Pallas kernels, gather_factors(): pl.pallas_call(functools.partial(fused_kernel, workers, replicas), out_sh...  71.2 us
    pallas_call x1, Pallas kernels, gather_factors(): pl.pallas_call(permute_kernel, out_shape=jax.ShapeDtypeStruct((blocks, sh...  5.18 us

profile of v4, /device:TPU:0, one launch (start us, length us, event | category | flops | bytes accessed | tf_op | source)
XLA Modules:
  0.0 79.9 jit_solution(10473409821506251803)
XLA Ops:
  0.0 0.7 broadcast_xor_fusion
  0.7 0.8 reshape.32
  1.4 0.8 reshape.31
  2.2 0.1 select_reduce_fusion.3
  2.3 0.1 select_reduce_fusion.2
  2.4 0.1 select_reduce_fusion.4
  2.4 0.2 convert_reduce_fusion.1
  2.6 0.0 copy-start
  2.6 0.2 convert_reduce_fusion
  2.8 0.7 select_reduce_fusion
  3.5 71.2 %shard_map.109.in_ref = bf16[32,128,512]{2,1,0:T(8,128)(2,1)} custom-call(s32[32]{0:T(128)} %get-tuple-element.6.first_ref, s32[32]{0:T(128)} %get-tuple-element.5.second_ref, bf16[32,512,128]{2,1,0:T(8,128)(2,1)} %g_hbm.1, bf16[1,32,512]{2,1,0:T(8,128)(2,1)} %os_ref.1, bf16[1,32,512]{2,1,0:T(8,128)(2,1)} %is_ref.1, f32[1,512,512]{2,1,0:T(8,128)} %of_hbm.1, ...), custom_call_target="tpu_custom_call" | custom-call | tf_op jit(solution)/shard_map/pallas_call | solution.py:428
  74.7 0.0 copy-done
  74.7 5.2 %shard_map.110 = bf16[32,128,512]{2,1,0:T(8,128)(2,1)} custom-call(s32[32]{0:T(128)} %copy-done, bf16[32,128,512]{2,1,0:T(8,128)(2,1)} %shard_map.109.in_ref), custom_call_target="tpu_custom_call" | custom-call | tf_op jit(solution)/shard_map/pallas_call | solution.py:471
  (3 shorter events, 0.0 us)
Async XLA Ops:
  2.6 72.1 %copy-start = (s32[32]{0:T(128)}, s32[32]{0:T(128)S(1)}, u32[]{:S(2)}) copy-start(s32[32]{0:T(128)S(1)} %multiply_add_fusion.1.place_ref) | copy-start | bytes 388
